TPU v7x, 32 devices: a whole 2x2x4 slice. The times are simulated.
32 devices in a mesh: tm: 8 (over z, x), head: 4 (over y, core).
Axes of the slice: x: 2, y: 2, z: 4, core: 2. Of those that a mesh axis runs over, the one named last changes fastest.
Arguments:
- query_rows: float32 [4096, 2240], P('tm', 'head'), may hold values from -6 to 6
- key_rows: float32 [4096, 2240], P('tm', 'head'), may hold values from -6 to 6
- value_rows: float32 [4096, 2240], P('tm', 'head'), may hold values from -6 to 6
- out_weight: float32 [2240, 2240], P(None, 'head'), may hold values from -0.125 to 0.125
- cotangent: float32 [4096, 2240], P('tm', 'head'), may hold values from -6 to 6
Outputs:
- grad_query: float32 [4096, 2240], P('tm', 'head')
- grad_key: float32 [4096, 2240], P('tm', 'head')
- grad_value: float32 [4096, 2240], P('tm', 'head')
- grad_weight: float32 [2240, 2240], P('tm', 'head')
All inputs are finite; a program needn't handle non-finite values.
Results may differ from a plain program's by a relative error of at most 0.0003.
Values sent between devices are 32-bit elements; how exact they have to be, the bound alone decides.
A program may use at most 128 MiB of HBM per device.

v0:
```python
import jax
import jax.numpy as jnp
from jax import lax
from jax.sharding import PartitionSpec as P

HEAD_DIM = 112


def prefix(part, axis, combine, identity, reverse):
    count = lax.axis_size(axis)
    place = lax.axis_index(axis)
    ahead = count - 1 - place if reverse else place
    gathered = jax.tree.map(lambda a: lax.all_gather(a, axis), part)
    state = jax.tree.map(lambda a, e: jnp.zeros_like(a) + jnp.asarray(e, a.dtype), part, identity)

    def one(lap, state):
        source = count - 1 - lap if reverse else lap
        return combine(
            state, jax.tree.map(lambda a: lax.dynamic_index_in_dim(a, source, 0, False), gathered)
        )

    return lax.fori_loop(0, ahead, one, state)


def add_pair(earlier, later):
    return (earlier[0] + later[0], earlier[1] + later[1])


def shards(query_rows, key_rows, value_rows, out_weight, cotangent):
    highest = lax.Precision.HIGHEST
    rows_here = query_rows.shape[0]
    width_here = query_rows.shape[1]
    heads_here = width_here // HEAD_DIM
    shape_heads = (rows_here, heads_here, HEAD_DIM)
    query_blk = query_rows.reshape(shape_heads)
    key_blk = key_rows.reshape(shape_heads)
    value_blk = value_rows.reshape(shape_heads)
    feat_q = jax.nn.relu(query_blk)
    feat_k = jax.nn.relu(key_blk)
    causal_mask = jnp.tril(jnp.ones((rows_here, rows_here), jnp.float32))
    local_state = jnp.einsum("thi,thj->hij", feat_k, value_blk, precision=highest)
    local_normal = jnp.sum(feat_k, axis=0)
    zero_state = jnp.zeros((heads_here, HEAD_DIM, HEAD_DIM), jnp.float32)
    zero_normal = jnp.zeros((heads_here, HEAD_DIM), jnp.float32)
    state, normal = prefix(
        (local_state, local_normal), "tm", add_pair, (zero_state, zero_normal), False
    )
    whole_grad = lax.all_gather(cotangent, "head", axis=1, tiled=True)
    grad_att = jnp.dot(
        whole_grad, out_weight, precision=highest, preferred_element_type=jnp.float32
    ).reshape(shape_heads)
    scores = jnp.einsum("thi,shi->hts", feat_q, feat_k, precision=highest) * causal_mask
    numer = jnp.einsum("hts,shj->thj", scores, value_blk, precision=highest)
    numer = numer + jnp.einsum("thi,hij->thj", feat_q, state, precision=highest)
    denom = (
        1.0
        + jnp.sum(scores, axis=-1).T
        + jnp.einsum("thi,hi->th", feat_q, normal, precision=highest)
    )
    attended = numer / denom[:, :, None]
    attended_flat = attended.reshape(rows_here, width_here)
    share_rows = whole_grad.shape[1] // lax.axis_size("tm")
    grad_num = grad_att / denom[:, :, None]
    grad_den = -jnp.sum(grad_att * attended, axis=-1) / denom
    local_back = jnp.einsum("thi,thj->hij", feat_q, grad_num, precision=highest)
    local_norm = jnp.einsum("th,thi->hi", grad_den, feat_q, precision=highest)
    back, back_norm = prefix(
        (local_back, local_norm), "tm", add_pair, (zero_state, zero_normal), True
    )
    grad_scores = (
        jnp.einsum("thj,shj->hts", grad_num, value_blk, precision=highest) + grad_den.T[:, :, None]
    ) * causal_mask
    grad_fq = jnp.einsum("hts,shi->thi", grad_scores, feat_k, precision=highest)
    grad_fq = (
        grad_fq
        + jnp.einsum("thj,hij->thi", grad_num, state, precision=highest)
        + grad_den[:, :, None] * normal[None]
    )
    grad_fk = jnp.einsum("hts,thi->shi", grad_scores, feat_q, precision=highest)
    grad_fk = (
        grad_fk + jnp.einsum("hij,shj->shi", back, value_blk, precision=highest) + back_norm[None]
    )
    grad_val = jnp.einsum("hts,thj->shj", scores, grad_num, precision=highest)
    grad_val = grad_val + jnp.einsum("shi,hij->shj", feat_k, back, precision=highest)
    grad_query = jnp.where(query_blk > 0, grad_fq, 0.0).reshape(rows_here, width_here)
    grad_key = jnp.where(key_blk > 0, grad_fk, 0.0).reshape(rows_here, width_here)
    grad_value = grad_val.reshape(rows_here, width_here)
    full_term = lax.dot_general(
        whole_grad,
        attended_flat,
        (((0,), (0,)), ((), ())),
        precision=highest,
        preferred_element_type=jnp.float32,
    )
    summed = lax.psum(full_term, "tm")
    grad_weight = lax.dynamic_slice_in_dim(summed, lax.axis_index("tm") * share_rows, share_rows, 0)
    return (grad_query, grad_key, grad_value, grad_weight)


def solution(mesh):
    return jax.shard_map(
        shards,
        mesh=mesh,
        in_specs=(
            P("tm", "head"),
            P("tm", "head"),
            P("tm", "head"),
            P(None, "head"),
            P("tm", "head"),
        ),
        out_specs=(P("tm", "head"), P("tm", "head"), P("tm", "head"), P("tm", "head")),
        check_vma=False,
    )
```

profile of v0, /device:TPU:0, one launch (start us, length us, event | category | flops | bytes accessed | tf_op | source)
XLA Modules:
  0.0 362.0 jit_solution(3450662816106841936)
XLA Ops:
  7.2 0.0 copy-start
  7.2 0.0 all-gather.10.cloned.1.call-start
  7.2 1.5 fusion.29
  8.8 0.0 copy-done
  8.8 1.0 copy-done.1
  9.8 1.9 fusion.33
  11.7 0.0 all-gather.10.cloned.1.call-update
  11.7 0.0 all-gather.8.cloned.1.call-start
  11.7 0.7 all-gather.8.cloned.1.call-update
  12.5 0.0 all-gather.12.cloned.1.call-start
  12.5 0.1 all_gather.30
  12.6 32.2 %all_gather.31 = f32[8,5,112]{2,1,0:T(8,128)S(1)} all-gather(f32[1,5,112]{2,1,0:T(8,128)S(1)} %all_gather.30), channel_id=1, replica_groups=mesh['tm'=8,'head'=4] {'tm'}, dimensions={0}, use_global_device_ids=true | all-gather | bytes 20160 | tf_op jit(solution)/shard_map/all_gather | solution.py:13
  44.8 0.1 fusion.23
  44.9 0.0 copy-start.2
  44.9 1.5 broadcast_maximum_fusion
  46.4 0.1 copy-done.2
  46.5 6.5 %multiply_reduce_fusion = (f32[5,512]{1,0:T(8,128)S(1)}, f32[5,512,512]{1,2,0:T(8,128)}) fusion(f32[512,512]{0,1:T(8,128)S(1)} %fusion.23, f32[512,5,112]{0,2,1:T(8,128)S(1)} %bitcast.94, f32[512,5,112]{0,2,1:T(8,128)S(1)} %bitcast.101), kind=kOutput, calls=%fused_computation.12 | convolution fusion | flops 1764226560 | bytes 8595456 | tf_op jit(solution)/shard_map/thi,shi->hts/dot_general | solution.py:52
  53.0 13.0 %all-gather.10.cloned.1.call-done = f32[40,112,112]{2,1,0:T(8,128)} async-done(((f32[5,112,112]{2,1,0:T(8,128)}), f32[40,112,112]{2,1,0:T(8,128)}) %all-gather.10.cloned.1.call-update) | async-done | bytes 2007056 | tf_op jit(solution)/shard_map/all_gather | solution.py:13
  66.0 0.7 broadcast_in_dim.26.clone
  66.7 0.6 fusion.27
  67.4 35.5 %all-gather.8.cloned.1.call-done = f32[512,2240]{0,1:T(8,128)} async-done(((f32[512,560]{0,1:T(8,128)}), f32[512,2240]{0,1:T(8,128)}) %all-gather.8.cloned.1.call-update) | async-done | bytes 4587536 | tf_op jit(solution)/shard_map/all_gather | solution.py:48
  102.8 10.7 %fusion.32 = f32[512,560]{0,1:T(8,128)S(1)} fusion(f32[512,2240]{0,1:T(8,128)} %all-gather.8.cloned.1.call-done, f32[2240,560]{0,1:T(8,128)} %param.12), kind=kOutput, calls=%fused_computation.53 | convolution fusion | flops 7707033600 | bytes 10752000 | tf_op jit(solution)/shard_map/dot_general | solution.py:49
  113.6 0.0 copy-start.5
  113.6 1.0 copy-done.5
  114.6 1.9 fusion.30
  116.5 0.0 all-gather.12.cloned.1.call-update
  116.6 0.2 all-reduce.2.cloned.1.call-start
  116.8 0.0 copy-start.10
  116.8 2.2 broadcast_compare_fusion
  119.0 0.9 broadcast_compare_fusion.1
  119.9 5.8 %fusion.13 = f32[512,5,112]{0,2,1:T(8,128)S(1)} fusion(f32[512,5,112]{0,2,1:T(8,128)S(1)} %bitcast.90, f32[5,512,512]{1,2,0:T(8,128)} %get-tuple-element.162, f32[512,512]{0,1:T(8,128)S(1)} %fusion.23), kind=kOutput, calls=%fused_computation.23 | convolution fusion | flops 1762918400 | bytes 8585216 | tf_op jit(solution)/shard_map/hts,shj->thj/dot_general | solution.py:53
  125.7 0.0 copy-done.6
  125.8 0.0 copy-done.8
  125.8 1.3 multiply_reduce_fusion.1
  127.2 10.4 %convolution_bitcast_fusion = f32[2240,560]{0,1:T(8,128)} fusion(f32[512,560]{0,1:T(8,128)S(1)} %bitcast.111, f32[512,2240]{0,1:T(8,128)S(1)} %bitcast.105), kind=kOutput, calls=%fused_computation.5 | convolution fusion | flops 7707033600 | bytes 10752000 | tf_op jit(solution)/shard_map/dot_general | solution.py:88
  137.5 0.0 all-reduce.2.cloned.1.call-update
  137.5 0.0 copy-start.7
  137.6 1.0 fusion.24
  138.6 31.0 %all-gather.3 = f32[8,5,112]{2,1,0:T(8,128)S(1)} all-gather(f32[1,5,112]{2,1,0:T(8,128)S(1)} %bitcast.120), channel_id=4, replica_groups=mesh['tm'=8,'head'=4] {'tm'}, dimensions={0}, use_global_device_ids=true | all-gather | bytes 20160 | tf_op jit(solution)/shard_map/all_gather | solution.py:13
  169.6 0.0 copy-start.3
  169.6 4.3 %fusion.31 = f32[5,512,512]{1,2,0:T(8,128)S(1)} fusion(f32[512,5,112]{0,2,1:T(8,128)S(1)} %bitcast.89, f32[512,5,112]{0,2,1:T(8,128)S(1)} %bitcast.108, f32[512,5]{0,1:T(8,128)S(1)} %fusion.26), kind=kOutput, calls=%fused_computation.52 | convolution fusion | flops 1761894400 | bytes 7546880 | tf_op jit(solution)/shard_map/thj,shj->hts/dot_general | solution.py:71
  174.0 0.0 copy-start.9
  174.0 0.0 copy-start.13
  174.0 3.3 fusion.1
  177.3 0.0 copy-done.9
  177.3 0.0 copy-done.13
  177.3 0.0 slice-start
  177.3 2.3 fusion.17
  179.6 6.6 %fusion = f32[5,112,512]{2,1,0:T(8,128)} fusion(f32[512,5,112]{0,2,1:T(8,128)S(1)} %bitcast.99, f32[5,512,512]{1,2,0:T(8,128)S(1)} %fusion.31, f32[5,512]{1,0:T(8,128)S(1)} %bitcast_divide_fusion, f32[512,512]{0,1:T(8,128)S(1)} %fusion.23), kind=kOutput, calls=%fused_computation.6 | convolution fusion | flops 1764229120 | bytes 8595456 | tf_op jit(solution)/shard_map/hts,thi->shi/dot_general | solution.py:79
  186.2 6.3 %fusion.2 = f32[5,112,512]{2,1,0:T(8,128)} fusion(f32[5,512,512]{1,2,0:T(8,128)S(1)} %bitcast.93, f32[512,512]{0,1:T(8,128)S(1)} %fusion.23, f32[512,5,112]{0,2,1:T(8,128)S(1)} %bitcast.110, f32[512,5]{0,1:T(8,128)S(1)} %fusion.26), kind=kOutput, calls=%fused_computation.8 | convolution fusion | flops 1763205120 | bytes 8595456 | tf_op jit(solution)/shard_map/hts,thj->shj/dot_general | solution.py:83
  192.5 7.5 %while.27 = (s32[]{:T(128)}, f32[5,112,112]{2,1,0:T(8,128)S(1)}, f32[5,112]{1,0:T(8,128)S(1)}, s32[]{:T(128)}, f32[8,5,112,112]{3,2,1,0:T(8,128)}, /*index=5*/f3...) while((s32[]{:T(128)}, f32[5,112,112]{2,1,0:T(8,128)S(1)}, f32[5,112]{1,0:T(8,128)S(1)}, ...), condition=%wide.region_6.7_spmd, body=%wide.region_5.6_spmd.sunk | while | flops 63286 | bytes 759515 | solution.py:22
  192.6 1.0 bitcast_add_fusion.11
  193.6 1.0 bitcast_add_fusion.11
  194.7 1.0 bitcast_add_fusion.11
  195.8 1.0 bitcast_add_fusion.11
  196.8 1.0 bitcast_add_fusion.11
  197.9 1.0 bitcast_add_fusion.11
  198.9 1.0 bitcast_add_fusion.11
  200.0 0.0 copy-start.11
  200.0 3.5 convolution_add_fusion
  203.6 2.2 fusion.20
  205.7 146.6 %all-reduce.2.cloned.1.call-done = f32[2240,560]{0,1:T(8,128)} async-done(((f32[2240,560]{0,1:T(8,128)}), f32[2240,560]{0,1:T(8,128)}) %all-reduce.2.cloned.1.call-update) | async-done | bytes 5017616 | tf_op jit(solution)/shard_map/psum | solution.py:95
  352.4 1.5 constant_dynamic-slice_fusion
  353.9 1.2 copy.32
  (36 shorter events, 0.2 us)
Async XLA Ops:
  7.2 1.6 copy-start
  7.2 58.8 %all-gather.10.cloned.1.call-start = ((), (), s32[]{:S(2)}) async-start(), calls=%async_computation.2 | async-start | bytes 2580480 | tf_op jit(solution)/shard_map/all_gather | solution.py:13
  8.8 1.0 copy-start.1
  11.7 91.1 %all-gather.8.cloned.1.call-start = ((), (), s32[]{:S(2)}) async-start(), calls=%async_computation | async-start | bytes 5734400 | tf_op jit(solution)/shard_map/all_gather | solution.py:48
  12.5 180.0 %all-gather.12.cloned.1.call-start = ((), (), s32[]{:S(2)}) async-start(), calls=%async_computation.3 | async-start | bytes 2580480 | tf_op jit(solution)/shard_map/all_gather | solution.py:13
  44.9 1.6 copy-start.2
  113.6 1.0 copy-start.5
  116.6 235.8 %all-reduce.2.cloned.1.call-start = ((), (), s32[]{:S(2)}) async-start(), calls=%async_computation.1 | async-start | bytes 10321920 | tf_op jit(solution)/shard_map/psum | solution.py:95
  116.8 2.2 copy-start.10
  119.9 7.2 %slice-start.2 = ((s8[4587520]{0:T(1024)(128)(4,1)}), s8[4194304]{0:T(1024)(128)(4,1)S(1)}, s32[]{:S(2)}) async-start(s8[4587520]{0:T(1024)(128)(4,1)} %bitcast.104), calls=%async_computation.6 | async-start | bytes 8388608
  119.9 5.9 %copy-start.6 = (f32[512,560]{0,1:T(8,128)S(1)}, f32[512,560]{0,1:T(8,128)}, u32[]{:S(2)}) copy-start(f32[512,560]{0,1:T(8,128)} %copy-done.5) | copy-start | bytes 3440644
  119.9 5.9 %copy-start.8 = (f32[5,112,112]{2,1,0:T(8,128)S(1)}, f32[5,112,112]{2,1,0:T(8,128)}, u32[]{:S(2)}) copy-start(f32[5,112,112]{2,1,0:T(8,128)} %get-tuple-element.120) | copy-start | bytes 752644
  119.9 7.2 %slice-start.3 = ((s8[4587520]{0:T(1024)(128)(4,1)}), s8[393216]{0:T(1024)(128)(4,1)S(1)}, s32[]{:S(2)}) async-start(s8[4587520]{0:T(1024)(128)(4,1)} %bitcast.104), calls=%async_computation.7 | async-start | bytes 786432
  137.5 32.1 %copy-start.7 = (f32[512,560]{0,1:T(8,128)S(1)}, f32[512,560]{0,1:T(8,128)}, u32[]{:S(2)}) copy-start(f32[512,560]{0,1:T(8,128)} %copy-done.5) | copy-start | bytes 3440644
  169.6 4.3 %copy-start.3 = (f32[512,560]{0,1:T(8,128)S(1)}, f32[512,560]{0,1:T(8,128)}, u32[]{:S(2)}) copy-start(f32[512,560]{0,1:T(8,128)} %copy-done.1) | copy-start | bytes 3440644
  174.0 3.4 copy-start.9
  174.0 3.4 copy-start.13
  177.3 8.9 %slice-start = ((s8[5242880]{0:T(1024)(128)(4,1)}), s8[4194304]{0:T(1024)(128)(4,1)S(1)}, s32[]{:S(2)}) async-start(s8[5242880]{0:T(1024)(128)(4,1)} %bitcast.92), calls=%async_computation.4 | async-start | bytes 8388608
  179.6 6.6 %slice-start.1 = ((s8[5242880]{0:T(1024)(128)(4,1)}), s8[1048576]{0:T(1024)(128)(4,1)S(1)}, s32[]{:S(2)}) async-start(s8[5242880]{0:T(1024)(128)(4,1)} %bitcast.92), calls=%async_computation.5 | async-start | bytes 2097152
  186.2 13.8 %copy-start.4 = (f32[512,560]{0,1:T(8,128)S(1)}, f32[512,560]{0,1:T(8,128)}, u32[]{:S(2)}) copy-start(f32[512,560]{0,1:T(8,128)} %copy-done.1) | copy-start | bytes 3440644
  200.0 3.5 copy-start.11
  200.0 3.5 copy-start.12
Sparse Core Ops, SparseCore 0:
  11.8 54.1 all-gather.9
  67.5 35.2 all-gather.7
  116.7 51.6 all-gather.11
  171.9 180.4 all-reduce.1
where the time goes:
time: 369 us; the launch traced here: 362 us
  waiting for transfers between devices  196 us (53%)
  matrix products  68.8 us (19%)
  blocking collectives  63.2 us (17%)
  between operations  14.5 us (4%)
  other arithmetic  13.4 us (4%)
  local copies, waits for them, and re-layouts  5.75 us (2%)
    psum x1, waiting for transfers between devices, shards(): summed = lax.psum(full_term, 'tm')  147 us
    all_gather x2, blocking collectives, prefix(): gathered = jax.tree.map(lambda a: lax.all_gather(a, axis), part)  63.2 us
    all_gather x1, waiting for transfers between devices, shards(): whole_grad = lax.all_gather(cotangent, 'head', axis=1, tiled=True)  35.5 us
    all_gather x2, waiting for transfers between devices, prefix(): gathered = jax.tree.map(lambda a: lax.all_gather(a, axis), part)  13 us
    dot_general x1, matrix products, shards(): jnp.dot(whole_grad, out_weight, precision=highest, preferred_element_type...  10.7 us
    dot_general x1, matrix products, shards(): lax.dot_general(whole_grad, attended_flat, (((0,), (0,)), ((), ())), prec...  10.4 us
  transfers between devices with their start and end apart: 4, of which 3 were waited for; matrix products, arithmetic and copies ran while one was open for 18% of the time, Pallas kernels for 0%

commit v1 on v0

v1 whole, which is shorter than its diff:
```python
import jax
import jax.numpy as jnp
from jax import lax
from jax.sharding import PartitionSpec as P

HEAD_DIM = 112
HIGH = lax.Precision.HIGH


def ein(spec, a, b):
    return jnp.einsum(spec, a, b, precision=HIGH, preferred_element_type=jnp.float32)


def prefix(part, axis, reverse):
    count = lax.axis_size(axis)
    place = lax.axis_index(axis)
    gathered = lax.all_gather(part, axis)
    index = lax.iota(jnp.int32, count)
    wanted = index > place if reverse else index < place
    return jnp.sum(jnp.where(wanted.reshape((count,) + (1,) * part.ndim), gathered, 0.0), axis=0)


def shards(query_rows, key_rows, value_rows, out_weight, cotangent):
    rows = query_rows.shape[0]
    width = query_rows.shape[1]
    heads = width // HEAD_DIM
    shape_heads = (rows, heads, HEAD_DIM)
    whole_grad = lax.all_gather(cotangent, "head", axis=1, tiled=True)
    query = query_rows.reshape(shape_heads).transpose(1, 0, 2)
    key = key_rows.reshape(shape_heads).transpose(1, 0, 2)
    value = value_rows.reshape(shape_heads).transpose(1, 0, 2)
    feat_q = jax.nn.relu(query)
    feat_k = jax.nn.relu(key)
    ones = jnp.ones((heads, rows, 1), jnp.float32)
    value_one = jnp.concatenate([value, ones], axis=2)
    mask = jnp.tril(jnp.ones((rows, rows), jnp.bool_))
    state = prefix(ein("hti,htj->hij", feat_k, value_one), "tm", False)
    scores = jnp.where(mask, ein("hti,hsi->hts", feat_q, feat_k), 0.0)
    both = ein("hts,hsj->htj", scores, value_one) + ein("hti,hij->htj", feat_q, state)
    denom = 1.0 + both[:, :, HEAD_DIM:]
    attended = both[:, :, :HEAD_DIM] / denom
    flat = attended.transpose(1, 0, 2).reshape(rows, width)
    term = lax.dot_general(
        whole_grad,
        flat,
        (((0,), (0,)), ((), ())),
        precision=HIGH,
        preferred_element_type=jnp.float32,
    )
    grad_weight = lax.psum_scatter(term, "tm", scatter_dimension=0, tiled=True)
    grad_att = jnp.dot(
        whole_grad, out_weight, precision=HIGH, preferred_element_type=jnp.float32
    )
    grad_att = grad_att.reshape(shape_heads).transpose(1, 0, 2)
    grad_num = grad_att / denom
    grad_den = -jnp.sum(grad_att * attended, axis=2, keepdims=True) / denom
    grad_one = jnp.concatenate([grad_num, grad_den], axis=2)
    back = prefix(ein("hti,htj->hij", feat_q, grad_one), "tm", True)
    grad_scores = jnp.where(mask, ein("htj,hsj->hts", grad_one, value_one), 0.0)
    grad_fq = ein("hts,hsi->hti", grad_scores, feat_k) + ein("htj,hij->hti", grad_one, state)
    grad_fk = ein("hts,hti->hsi", grad_scores, feat_q) + ein("hsj,hij->hsi", value_one, back)
    grad_val = ein("hts,htj->hsj", scores, grad_num) + ein(
        "hsi,hij->hsj", feat_k, back[:, :, :HEAD_DIM]
    )

    def merged(a):
        return a.transpose(1, 0, 2).reshape(rows, width)

    grad_query = merged(jnp.where(query > 0, grad_fq, 0.0))
    grad_key = merged(jnp.where(key > 0, grad_fk, 0.0))
    return (grad_query, grad_key, merged(grad_val), grad_weight)


def solution(mesh):
    return jax.shard_map(
        shards,
        mesh=mesh,
        in_specs=(
            P("tm", "head"),
            P("tm", "head"),
            P("tm", "head"),
            P(None, "head"),
            P("tm", "head"),
        ),
        out_specs=(P("tm", "head"), P("tm", "head"), P("tm", "head"), P("tm", "head")),
        check_vma=False,
    )
```

time: 369 us -> 357 us (0.967); the launches traced: 362 us -> 357 us
  waiting for transfers between devices: 196 us -> 276 us
  blocking collectives: 63.2 us -> 0 us
  matrix products: 68.8 us -> 46.3 us
    unnamed x4 -> x5, waiting for transfers between devices: 0.74 us -> 172 us
    psum x1 -> x0, waiting for transfers between devices: 147 us -> none  [shards(): summed = lax.psum(full_term, 'tm')]
    all_gather x2 -> x0, blocking collectives: 63.2 us -> none  [prefix(): gathered = jax.tree.map(lambda a: lax.all_gather(a, axis), part)]
    all_gather x2, waiting for transfers between devices: 13 us -> 76 us  [prefix(): gathered = lax.all_gather(part, axis)]
    dot_general x16 -> x14, matrix products: 68.8 us -> 46.3 us  [the longest x12 29.2 us: ein(): jnp.einsum(spec, a, b, precision=HIGH, preferred_element_type=jnp.float32)]
    add x15 -> x1, other arithmetic: 7.21 us -> 0.01 us  [shards(): denom = 1.0 + both[:, :, HEAD_DIM:]]
    all_gather x1, waiting for transfers between devices: 35.5 us -> 28.3 us  [shards(): whole_grad = lax.all_gather(cotangent, 'head', axis=1, tiled=True)]
    unnamed x37 -> x36, local copies, waits for them, and re-layouts: 3.37 us -> 7.49 us
  transfers between devices with their start and end apart: 4 -> 4, of which waited for: 3 -> 4; matrix products, arithmetic and copies ran while one was open for 18% -> 13% of each run, Pallas kernels for 0% -> 0%
where the time goes in v1:
time: 357 us
  waiting for transfers between devices  276 us (77%)
  matrix products  46.3 us (13%)
  between operations  14.7 us (4%)
  other arithmetic  11.5 us (3%)
  local copies, waits for them, and re-layouts  7.49 us (2%)
    unnamed x5, waiting for transfers between devices  172 us
    all_gather x2, waiting for transfers between devices, prefix(): gathered = lax.all_gather(part, axis)  76 us
    dot_general x12, matrix products, ein(): jnp.einsum(spec, a, b, precision=HIGH, preferred_element_type=jnp.float32)  29.2 us
    all_gather x1, waiting for transfers between devices, shards(): whole_grad = lax.all_gather(cotangent, 'head', axis=1, tiled=True)  28.3 us
    dot_general x1, matrix products, shards(): lax.dot_general(whole_grad, flat, (((0,), (0,)), ((), ())), precision=HIG...  9.29 us
    dot_general x1, matrix products, shards(): jnp.dot(whole_grad, out_weight, precision=HIGH, preferred_element_type=jn...  7.78 us
    unnamed x36, local copies, waits for them, and re-layouts  7.49 us
  transfers between devices with their start and end apart: 4, of which 4 were waited for; matrix products, arithmetic and copies ran while one was open for 13% of the time, Pallas kernels for 0%

profile of v1, /device:TPU:0, one launch (start us, length us, event | category | flops | bytes accessed | tf_op | source)
XLA Modules:
  0.0 356.7 jit_solution(8801673873086542397)
XLA Ops:
  7.2 0.0 copy-start.2
  7.2 0.0 all-gather.8.cloned.1.call-start
  7.2 1.5 broadcast_maximum_fusion
  8.7 0.1 copy-done.2
  8.8 1.4 fusion.44
  10.1 0.0 all-gather.8.cloned.1.call-update
  10.2 0.0 all-gather.6.cloned.1.call-start
  10.2 0.7 all-gather.6.cloned.1.call-update
  10.9 0.0 all-gather.10.cloned.1.call-start
  11.0 0.8 iota_compare_fusion
  11.8 1.4 broadcast_maximum_fusion.1
  13.1 4.6 %fusion.63 = f32[5,512,512]{2,1,0:T(8,128)} fusion(f32[5,512,112]{1,2,0:T(8,128)S(1)} %bitcast.62, f32[5,512,112]{1,2,0:T(8,128)S(1)} %bitcast.59), kind=kOutput, calls=%fused_computation.65 | convolution fusion | flops 880803840 | bytes 7536640 | tf_op jit(solution)/shard_map/hti,hsi->hts/dot_general | solution.py:11
  17.7 47.1 %all-gather.8.cloned.1.call-done = f32[40,112,113]{2,1,0:T(8,128)} async-done(((f32[5,112,113]{2,1,0:T(8,128)}), f32[40,112,113]{2,1,0:T(8,128)}) %all-gather.8.cloned.1.call-update) | async-done | bytes 2024976 | tf_op jit(solution)/shard_map/all_gather | solution.py:17
  64.8 2.1 select_reduce_fusion.1
  66.9 0.0 copy-start.10
  66.9 0.7 copy-done.10
  67.6 0.7 fusion.64
  68.3 0.0 copy-done
  68.4 3.9 %fusion.16 = f32[5,512,113]{1,2,0:T(8,128)S(1)} fusion(f32[5,512,113]{1,2,0:T(8,128)S(1)} %fusion.64, f32[5,512,512]{2,1,0:T(8,128)S(1)} %copy-done, pred[512,512]{1,0:T(8,128)(4,1)} %iota_compare_fusion, f32[5,512,112]{1,2,0:T(8,128)S(1)} %bitcast.67), kind=kOutput, calls=%fused_computation.19 | convolution fusion | flops 890268160 | bytes 8966144 | tf_op jit(solution)/shard_map/hts,hsj->htj/dot_general | solution.py:11
  72.3 0.0 copy-start.7
  72.3 1.0 copy-done.7
  73.3 28.3 %all-gather.6.cloned.1.call-done = f32[512,2240]{0,1:T(8,128)} async-done(((f32[512,560]{0,1:T(8,128)}), f32[512,2240]{0,1:T(8,128)}) %all-gather.6.cloned.1.call-update) | async-done | bytes 4587536 | tf_op jit(solution)/shard_map/all_gather | solution.py:28
  101.6 7.8 %fusion.62 = f32[512,560]{0,1:T(8,128)S(1)} fusion(f32[512,2240]{0,1:T(8,128)} %all-gather.6.cloned.1.call-done, f32[2240,560]{0,1:T(8,128)} %param.8), kind=kOutput, calls=%fused_computation.64 | convolution fusion | flops 3853516800 | bytes 10752000 | tf_op jit(solution)/shard_map/dot_general | solution.py:51
  109.4 0.0 copy-done.8
  109.4 1.3 multiply_reduce_fusion
  110.8 1.4 fusion.47
  112.2 0.0 all-gather.10.cloned.1.call-update
  112.2 0.2 all-reduce.4.cloned.1.call-start
  112.4 9.3 %convolution_bitcast_fusion = f32[2240,560]{0,1:T(8,128)} fusion(f32[512,560]{0,1:T(8,128)} %bitcast.70, f32[512,2240]{0,1:T(8,128)} %all-gather.6.cloned.1.call-done), kind=kOutput, calls=%fused_computation | convolution fusion | flops 3853516800 | bytes 10752000 | tf_op jit(solution)/shard_map/dot_general | solution.py:43
  121.7 0.0 all-reduce.4.cloned.1.call-update
  121.7 0.6 copy-done.13
  122.4 0.6 dynamic-slice
  123.6 0.0 copy-start.9
  123.6 0.0 copy-start.3
  123.6 2.3 broadcast_compare_fusion
  125.9 0.0 copy-done.9
  125.9 0.2 broadcast_compare_fusion.1
  126.1 0.0 copy-done.3
  126.1 0.0 copy-start.11
  126.1 2.4 fusion.42
  128.5 0.0 copy-done.11
  128.5 0.0 copy-start.1
  128.5 0.0 copy-start.5
  128.5 0.6 fusion.48
  129.2 1.7 copy-done.1
  130.8 0.0 copy-done.5
  130.9 3.9 %fusion.34 = f32[512,5,112]{0,2,1:T(8,128)} fusion(pred[512,5,112]{0,2,1:T(8,128)(4,1)S(1)} %bitcast.78, f32[5,512,112]{1,2,0:T(8,128)S(1)} %fusion.48, f32[5,512,112]{1,2,0:T(8,128)S(1)} %bitcast.60, f32[5,512,512]{2,1,0:T(8,128)S(1)} %fusion.42, pred[512,512]{1,0:T(8,128)(4,1)S(1)} %copy-done.5), kind=kOutput, calls=%fused_computation.25 | convolution fusion | flops 882688000 | bytes 9232384 | tf_op jit(solution)/shard_map/hts,hsi->hti/dot_general | solution.py:11
  134.8 28.9 %all-gather.10.cloned.1.call-done = f32[40,112,113]{2,1,0:T(8,128)} async-done(((f32[5,112,113]{2,1,0:T(8,128)}), f32[40,112,113]{2,1,0:T(8,128)}) %all-gather.10.cloned.1.call-update) | async-done | bytes 2024976 | tf_op jit(solution)/shard_map/all_gather | solution.py:17
  163.6 2.1 select_reduce_fusion
  165.7 0.0 copy-done.4
  165.7 0.0 copy-start.6
  165.7 0.6 fusion.40
  166.4 0.0 slice-start
  166.4 0.7 fusion.49
  167.1 0.0 copy-done.6
  167.1 0.0 slice-start.1
  167.1 0.0 copy-start.12
  167.1 6.0 %fusion.19 = f32[5,512,112]{1,2,0:T(8,128)} fusion(f32[5,512,112]{1,2,0:T(8,128)S(1)} %fusion.49, f32[5,512,112]{1,2,0:T(8,128)S(1)} %get-tuple-element.14, f32[5,512,512]{2,1,0:T(8,128)} %fusion.63, pred[512,512]{1,0:T(8,128)(4,1)S(1)} %copy-done.6), kind=kOutput, calls=%fused_computation.20 | convolution fusion | flops 882401280 | bytes 8945664 | tf_op jit(solution)/shard_map/hts,htj->hsj/dot_general | solution.py:11
  173.1 0.0 slice-done
  173.1 0.0 slice-done.1
  173.1 3.0 fusion.37
  176.1 171.3 %all-reduce.4.cloned.1.call-done = f32[2240,560]{0,1:T(8,128)} async-done(((f32[2240,560]{0,1:T(8,128)}), f32[2240,560]{0,1:T(8,128)}) %all-reduce.4.cloned.1.call-update) | async-done | bytes 5017616
  347.5 1.5 constant_dynamic-slice_fusion
  349.0 1.2 copy.12
  (12 shorter events, 0.1 us)
Async XLA Ops:
  7.2 1.6 copy-start.2
  7.2 57.6 %all-gather.8.cloned.1.call-start = ((), (), s32[]{:S(2)}) async-start(), calls=%async_computation.1 | async-start | bytes 2580480 | tf_op jit(solution)/shard_map/all_gather | solution.py:17
  10.2 91.5 %all-gather.6.cloned.1.call-start = ((), (), s32[]{:S(2)}) async-start(), calls=%async_computation | async-start | bytes 5734400 | tf_op jit(solution)/shard_map/all_gather | solution.py:28
  10.9 152.7 %all-gather.10.cloned.1.call-start = ((), (), s32[]{:S(2)}) async-start(), calls=%async_computation.2 | async-start | bytes 2580480 | tf_op jit(solution)/shard_map/all_gather | solution.py:17
  64.8 3.6 copy-start
  66.9 0.7 copy-start.10
  72.3 1.0 copy-start.7
  101.6 7.8 %copy-start.8 = (f32[5,512,113]{1,2,0:T(8,128)S(1)}, f32[5,512,113]{1,2,0:T(8,128)}, u32[]{:S(2)}) copy-start(f32[5,512,113]{1,2,0:T(8,128)} %copy-done.7) | copy-start | bytes 3471364
  112.2 235.3 %all-reduce.4.cloned.1.call-start = ((), (), s32[]{:S(2)}) async-start(), calls=%async_computation.3 | async-start | bytes 10321920
  121.7 0.7 copy-start.13
  123.6 2.3 copy-start.9
  123.6 2.4 copy-start.3
  126.1 2.4 copy-start.11
  128.5 2.4 copy-start.1
  128.5 2.4 copy-start.5
  163.6 2.1 copy-start.4
  165.7 1.3 copy-start.6
  166.4 6.7 %slice-start = ((s8[5242880]{0:T(1024)(128)(4,1)}), s8[4194304]{0:T(1024)(128)(4,1)S(1)}, s32[]{:S(2)}) async-start(s8[5242880]{0:T(1024)(128)(4,1)} %bitcast.56), calls=%async_computation.4 | async-start | bytes 8388608
  167.1 6.0 %slice-start.1 = ((s8[5242880]{0:T(1024)(128)(4,1)}), s8[1048576]{0:T(1024)(128)(4,1)S(1)}, s32[]{:S(2)}) async-start(s8[5242880]{0:T(1024)(128)(4,1)} %bitcast.56), calls=%async_computation.5 | async-start | bytes 2097152
  167.1 6.0 %copy-start.12 = (pred[512,560]{0,1:T(8,128)(4,1)S(1)}, pred[512,560]{0,1:T(8,128)(4,1)}, u32[]{:S(2)}) copy-start(pred[512,560]{0,1:T(8,128)(4,1)} %broadcast_compare_fusion) | copy-start | bytes 860164
Sparse Core Ops, SparseCore 0:
  10.8 53.9 all-gather.7
  66.4 35.2 all-gather.5
  112.3 51.2 all-gather.9
  167.2 180.2 all-reduce.3
